TPU v7x, 32 devices: a whole 2x2x4 slice. The times are simulated.
32 devices in a mesh: dir: 4 (over y, x), adj: 8 (over z, core).
Axes of the slice: x: 2, y: 2, z: 4, core: 2. Of those that a mesh axis runs over, the one named last changes fastest.
Arguments:
- direct_snapshots: bfloat16 [4096, 4096], P('dir', 'adj'), may hold values from -6 to 6
- adjoint_snapshots: bfloat16 [4096, 4096], P('dir', 'adj'), may hold values from -6 to 6
- start_seeds: int32 [512], replicated, may hold values from 0 to 65520
Outputs:
- balancing_modes: float32 [4096, 512], P(('dir', 'adj'))
- adjoint_modes: float32 [4096, 512], P(('dir', 'adj'))
All inputs are finite; a program needn't handle non-finite values.
Results may differ from a plain program's by a relative error of at most 0.0019.
Values may be sent and summed in bfloat16 or wider, within the bound.
A program may use at most 128 MiB of HBM per device.

v0:
```python
import jax
import jax.numpy as jnp
from jax import lax
from jax.sharding import PartitionSpec as P

ITERS = 2


def start_block(start_seeds, offset, length):
    row_col = (offset + jnp.arange(length, dtype=jnp.int32))[:, None]
    seed_row = start_seeds[None, :]
    col_ids = jnp.arange(start_seeds.shape[0], dtype=jnp.int32)[None, :] + 1
    column_term = (row_col + 1) * (col_ids * col_ids % 65521) % 65521
    hashed = (
        row_col * row_col % 65521 * (seed_row % 997 + 1) + 31 * seed_row + 7 * row_col + column_term
    ) % 65521
    return hashed.astype(jnp.float32) / 65521.0 - 0.5


def gram_of(block_rows):
    return lax.dot_general(
        block_rows,
        block_rows,
        (((0,), (0,)), ((), ())),
        precision=lax.Precision.HIGHEST,
        preferred_element_type=jnp.float32,
    )


def normalize(raw_block, gram_matrix):
    factor = jnp.linalg.cholesky(gram_matrix)
    return lax.linalg.triangular_solve(
        factor, raw_block, left_side=False, lower=True, transpose_a=True
    )


def reduce_adj(partial_value):
    summed = lax.psum(partial_value, "adj")
    gram_matrix = lax.psum(gram_of(summed), "dir")
    return normalize(summed, gram_matrix)


def reduce_dir(partial_value):
    summed = lax.psum(partial_value, "dir")
    gram_matrix = lax.psum(gram_of(summed), "adj")
    return normalize(summed, gram_matrix)


def product(matrix, block_rows):
    return jnp.dot(
        matrix, block_rows, precision=lax.Precision.HIGHEST, preferred_element_type=jnp.float32
    )


def product_back(matrix, block_rows):
    return lax.dot_general(
        matrix,
        block_rows,
        (((0,), (0,)), ((), ())),
        precision=lax.Precision.HIGHEST,
        preferred_element_type=jnp.float32,
    )


def local(direct_snapshots, adjoint_snapshots, start_seeds):
    adj_count = lax.axis_size("adj")
    adj_index = lax.axis_index("adj")
    share_rows = direct_snapshots.shape[0] // adj_count
    gathered = lax.all_gather(adjoint_snapshots, "adj", axis=1, tiled=True)
    hankel_tile = lax.psum_scatter(
        lax.dot_general(
            gathered, direct_snapshots, (((0,), (0,)), ((), ())), preferred_element_type=jnp.float32
        ),
        "dir",
        scatter_dimension=0,
        tiled=True,
    )
    right_basis = start_block(
        start_seeds, adj_index * direct_snapshots.shape[1], direct_snapshots.shape[1]
    )
    left_basis = jnp.zeros((hankel_tile.shape[0], right_basis.shape[1]), jnp.float32)
    for sweep in range(ITERS):
        left_basis = reduce_adj(product(hankel_tile, right_basis))
        right_basis = reduce_dir(product_back(hankel_tile, left_basis))
    right_coarse = right_basis.astype(jnp.bfloat16)
    balancing_modes = lax.psum_scatter(
        jnp.dot(direct_snapshots, right_coarse, preferred_element_type=jnp.float32),
        "adj",
        scatter_dimension=0,
        tiled=True,
    )
    left_whole = lax.all_gather(left_basis.astype(jnp.bfloat16), "dir", axis=0, tiled=True)
    own_rows = lax.dynamic_slice_in_dim(gathered, adj_index * share_rows, share_rows, 0)
    adjoint_modes = jnp.dot(own_rows, left_whole, preferred_element_type=jnp.float32)
    return (balancing_modes, adjoint_modes)


def solution(mesh):
    placed = (P("dir", "adj"), P("dir", "adj"), P())
    return jax.shard_map(
        local,
        mesh=mesh,
        in_specs=placed,
        out_specs=(P(("dir", "adj"), None), P(("dir", "adj"), None)),
        check_vma=False,
    )
```

profile of v0, /device:TPU:0, one launch (start us, length us, event | category | flops | bytes accessed | tf_op | source)
XLA Modules:
  0.0 1450.7 jit_solution(1376060498704825059)
XLA Ops:
  8.0 86.5 %all-gather.3.cloned.1.call-done = bf16[1024,4096]{1,0:T(8,128)(2,1)} async-done(((bf16[1024,512]{1,0:T(8,128)(2,1)}), bf16[1024,4096]{1,0:T(8,128)(2,1)}) %all-gather.3.cloned.1.call-update) | async-done | bytes 8388624 | tf_op jit(solution)/shard_map/all_gather | solution.py:69
  105.4 84.4 %reduce-scatter.3.cloned.1.call-done = f32[1024,512]{1,0:T(8,128)} async-done(((f32[4096,512]{1,0:T(8,128)}), f32[1024,512]{1,0:T(8,128)}) %reduce-scatter.3.cloned.1.call-update) | async-done | bytes 2097168 | tf_op jit(solution)/shard_map/reduce_scatter | solution.py:70
  197.7 65.0 %all-reduce.10.cloned.1.call-done = f32[1024,512]{1,0:T(8,128)} async-done(((f32[1024,512]{1,0:T(8,128)}), f32[1024,512]{1,0:T(8,128)}) %all-reduce.10.cloned.1.call-update) | async-done | bytes 2097168 | tf_op jit(solution)/shard_map/psum | solution.py:38
  269.7 52.1 %all-reduce.12.cloned.1.call-done = f32[512,512]{0,1:T(8,128)} async-done(((f32[512,512]{0,1:T(8,128)}), f32[512,512]{0,1:T(8,128)}) %all-reduce.12.cloned.1.call-update) | async-done | bytes 1048592 | tf_op jit(solution)/shard_map/psum | solution.py:39
  324.7 11.7 cholesky.462
  348.9 11.7 cholesky.481
  374.7 11.7 cholesky.502
  399.8 11.7 cholesky.519
  418.7 14.2 while.8
  432.9 40.8 %custom-call.40 = f32[4,128,128]{1,2,0:T(8,128)} custom-call(f32[4,128,128]{2,1,0:T(8,128)} %get-tuple-element.33), custom_call_target="InvertDiagBlocksLowerTriangular" | custom-call | tf_op jit(solution)/shard_map/triangular_solve/custom-call.3 | solution.py:32
  494.0 52.6 %all-reduce.14.cloned.1.call-done = f32[512,512]{1,0:T(8,128)} async-done(((f32[512,512]{1,0:T(8,128)}), f32[512,512]{1,0:T(8,128)}) %all-reduce.14.cloned.1.call-update) | async-done | bytes 1048592 | tf_op jit(solution)/shard_map/psum | solution.py:44
  551.3 58.9 %all-reduce.16.cloned.1.call-done = f32[512,512]{0,1:T(8,128)} async-done(((f32[512,512]{0,1:T(8,128)}), f32[512,512]{0,1:T(8,128)}) %all-reduce.16.cloned.1.call-update) | async-done | bytes 1048592 | tf_op jit(solution)/shard_map/psum | solution.py:45
  615.5 11.7 cholesky.534
  641.4 11.7 cholesky.553
  667.4 11.7 cholesky.574
  692.5 11.7 cholesky.591
  711.5 14.0 while.9
  725.5 40.8 %custom-call.44 = f32[4,128,128]{1,2,0:T(8,128)} custom-call(f32[4,128,128]{2,1,0:T(8,128)} %get-tuple-element.34), custom_call_target="InvertDiagBlocksLowerTriangular" | custom-call | tf_op jit(solution)/shard_map/triangular_solve/custom-call.8 | solution.py:32
  780.7 64.0 %all-reduce.18.cloned.1.call-done = f32[1024,512]{1,0:T(8,128)} async-done(((f32[1024,512]{1,0:T(8,128)}), f32[1024,512]{1,0:T(8,128)}) %all-reduce.18.cloned.1.call-update) | async-done | bytes 2097168 | tf_op jit(solution)/shard_map/psum | solution.py:38
  851.7 52.1 %all-reduce.20.cloned.1.call-done = f32[512,512]{0,1:T(8,128)} async-done(((f32[512,512]{0,1:T(8,128)}), f32[512,512]{0,1:T(8,128)}) %all-reduce.20.cloned.1.call-update) | async-done | bytes 1048592 | tf_op jit(solution)/shard_map/psum | solution.py:39
  909.1 11.7 cholesky.606
  934.9 11.7 cholesky.625
  961.2 11.7 cholesky.646
  986.3 11.7 cholesky.663
  1005.2 14.2 while.10
  1019.4 40.8 %custom-call.48 = f32[4,128,128]{1,2,0:T(8,128)} custom-call(f32[4,128,128]{2,1,0:T(8,128)} %get-tuple-element.35), custom_call_target="InvertDiagBlocksLowerTriangular" | custom-call | tf_op jit(solution)/shard_map/triangular_solve/custom-call.3 | solution.py:32
  1082.1 52.6 %all-reduce.22.cloned.1.call-done = f32[512,512]{1,0:T(8,128)} async-done(((f32[512,512]{1,0:T(8,128)}), f32[512,512]{1,0:T(8,128)}) %all-reduce.22.cloned.1.call-update) | async-done | bytes 1048592 | tf_op jit(solution)/shard_map/psum | solution.py:44
  1139.3 58.9 %all-reduce.24.cloned.1.call-done = f32[512,512]{0,1:T(8,128)} async-done(((f32[512,512]{0,1:T(8,128)}), f32[512,512]{0,1:T(8,128)}) %all-reduce.24.cloned.1.call-update) | async-done | bytes 1048592 | tf_op jit(solution)/shard_map/psum | solution.py:45
  1289.9 11.9 while.11
  1301.8 39.3 %custom-call.52 = f32[4,128,128]{1,2,0:T(8,128)S(1)} custom-call(f32[4,128,128]{2,1,0:T(8,128)S(1)} %get-tuple-element.36), custom_call_target="InvertDiagBlocksLowerTriangular" | custom-call | tf_op jit(solution)/shard_map/triangular_solve/custom-call.8 | solution.py:32
  1352.9 32.7 %reduce-scatter.5.cloned.1.call-done = f32[128,512]{0,1:T(8,128)} async-done(((f32[1024,512]{0,1:T(8,128)}), f32[128,512]{0,1:T(8,128)}) %reduce-scatter.5.cloned.1.call-update) | async-done | bytes 262160 | tf_op jit(solution)/shard_map/reduce_scatter | solution.py:86
  1387.4 51.5 %all-gather.5.cloned.1.call-done = bf16[4096,512]{0,1:T(8,128)(2,1)} async-done(((bf16[1024,512]{0,1:T(8,128)(2,1)}), bf16[4096,512]{0,1:T(8,128)(2,1)}) %all-gather.5.cloned.1.call-update) | async-done | bytes 4194320 | tf_op jit(solution)/shard_map/all_gather | solution.py:92
  (272 shorter events, 411.6 us)
Async XLA Ops:
  7.2 87.3 %copy-start = (bf16[1024,512]{1,0:T(8,128)(2,1)S(1)}, bf16[1024,512]{1,0:T(8,128)(2,1)}, u32[]{:S(2)}) copy-start(bf16[1024,512]{1,0:T(8,128)(2,1)} %param.8) | copy-start | bytes 3145732
  7.2 87.2 %all-gather.3.cloned.1.call-start = ((), (), s32[]{:S(2)}) async-start(), calls=%async_computation.2 | async-start | bytes 9437184 | tf_op jit(solution)/shard_map/all_gather | solution.py:69
  7.9 182.0 %reduce-scatter.3.cloned.1.call-start = ((), (), s32[]{:S(2)}) async-start(), calls=%async_computation.3 | async-start | bytes 10485760 | tf_op jit(solution)/shard_map/reduce_scatter | solution.py:70
  104.8 157.9 %all-reduce.10.cloned.1.call-start = ((), (), s32[]{:S(2)}) async-start(), calls=%async_computation.4 | async-start | bytes 4194304 | tf_op jit(solution)/shard_map/psum | solution.py:38
  197.6 124.2 %all-reduce.12.cloned.1.call-start = ((), (), s32[]{:S(2)}) async-start(), calls=%async_computation.5 | async-start | bytes 2097152 | tf_op jit(solution)/shard_map/psum | solution.py:39
  269.4 277.2 %all-reduce.14.cloned.1.call-start = ((), (), s32[]{:S(2)}) async-start(), calls=%async_computation.6 | async-start | bytes 2097152 | tf_op jit(solution)/shard_map/psum | solution.py:44
  321.8 1.7 copy-start.15
  323.7 1.0 copy-start.17
  374.6 99.0 %copy-start.2 = (f32[1024,512]{1,0:T(8,128)S(1)}, f32[1024,512]{1,0:T(8,128)}, u32[]{:S(2)}) copy-start(f32[1024,512]{1,0:T(8,128)} %all-reduce.10.cloned.1.call-done) | copy-start | bytes 6291460
  473.6 3.4 copy-start.21
  481.1 4.7 copy-start.1
  494.0 116.2 %all-reduce.16.cloned.1.call-start = ((), (), s32[]{:S(2)}) async-start(), calls=%async_computation.7 | async-start | bytes 2097152 | tf_op jit(solution)/shard_map/psum | solution.py:45
  551.2 293.4 %all-reduce.18.cloned.1.call-start = ((), (), s32[]{:S(2)}) async-start(), calls=%async_computation.8 | async-start | bytes 4194304 | tf_op jit(solution)/shard_map/psum | solution.py:38
  766.2 4.4 copy-start.9
  766.2 6.3 copy-start.22
  780.6 123.1 %all-reduce.20.cloned.1.call-start = ((), (), s32[]{:S(2)}) async-start(), calls=%async_computation.9 | async-start | bytes 2097152 | tf_op jit(solution)/shard_map/psum | solution.py:39
  851.5 283.2 %all-reduce.22.cloned.1.call-start = ((), (), s32[]{:S(2)}) async-start(), calls=%async_computation.10 | async-start | bytes 2097152 | tf_op jit(solution)/shard_map/psum | solution.py:44
  908.1 1.0 copy-start.19
  1060.1 4.2 copy-start.23
  1060.1 4.8 copy-start.3
  1062.0 11.0 copy-start.4
  1064.9 8.1 copy-start.6
  1068.5 4.6 copy-start.10
  1082.0 116.2 %all-reduce.24.cloned.1.call-start = ((), (), s32[]{:S(2)}) async-start(), calls=%async_computation.11 | async-start | bytes 2097152 | tf_op jit(solution)/shard_map/psum | solution.py:45
  1139.3 246.3 %reduce-scatter.5.cloned.1.call-start = ((), (), s32[]{:S(2)}) async-start(), calls=%async_computation.12 | async-start | bytes 2359296 | tf_op jit(solution)/shard_map/reduce_scatter | solution.py:86
  1198.3 1.7 copy-start.16
  1250.0 91.2 %copy-start.8 = (f32[512,512]{1,0:T(8,128)S(1)}, f32[512,512]{1,0:T(8,128)}, u32[]{:S(2)}) copy-start(f32[512,512]{1,0:T(8,128)} %all-reduce.22.cloned.1.call-done) | copy-start | bytes 3145732
  1348.6 2.2 copy-start.5
  1348.6 2.2 copy-start.7
  1348.6 2.2 copy-start.11
  1350.7 1.0 copy-start.14
  1350.7 88.2 %all-gather.5.cloned.1.call-start = ((), (), s32[]{:S(2)}) async-start(), calls=%async_computation.13 | async-start | bytes 5242880 | tf_op jit(solution)/shard_map/all_gather | solution.py:92
  (5 other events, 4.4 us)
Sparse Core Ops, SparseCore 0:
  9.6 84.7 all-gather.2
  104.9 84.9 reduce-scatter.2
  197.7 64.8 all-reduce.9
  269.6 52.1 all-reduce.11
  494.1 52.5 all-reduce.13
  551.4 58.7 all-reduce.15
  780.8 63.8 all-reduce.17
  851.6 52.1 all-reduce.19
  1082.2 52.4 all-reduce.21
  1139.4 58.8 all-reduce.23
  1350.9 34.6 reduce-scatter.4
  1387.4 51.4 all-gather.4
where the time goes:
time: 1460 us; the launch traced here: 1450 us
  waiting for transfers between devices  712 us (49%)
  other arithmetic  498 us (34%)
  matrix products  138 us (9%)
  local copies, waits for them, and re-layouts  76.2 us (5%)
  between operations  25.6 us (2%)
    another operation x60, other arithmetic, normalize(): factor = jnp.linalg.cholesky(gram_matrix)  322 us
    another operation x9, other arithmetic, normalize(): lax.linalg.triangular_solve(factor, raw_block, left_side=False, lower=Tru...  171 us
    psum x2, waiting for transfers between devices, reduce_adj(): summed = lax.psum(partial_value, 'adj')  129 us
    psum x2, waiting for transfers between devices, reduce_dir(): gram_matrix = lax.psum(gram_of(summed), 'adj')  118 us
    psum x2, waiting for transfers between devices, reduce_dir(): summed = lax.psum(partial_value, 'dir')  105 us
    psum x2, waiting for transfers between devices, reduce_adj(): gram_matrix = lax.psum(gram_of(summed), 'dir')  104 us
    all_gather x1, waiting for transfers between devices, local(): gathered = lax.all_gather(adjoint_snapshots, 'adj', axis=1, tiled=True)  86.5 us
    reduce_scatter x1, waiting for transfers between devices, local(): lax.psum_scatter(lax.dot_general(gathered, direct_snapshots, (((0,), (0,)...  84.4 us
  transfers between devices with their start and end apart: 12, of which 12 were waited for; matrix products, arithmetic and copies ran while one was open for 0% of the time, Pallas kernels for 0%

commit v1 on v0

v1 whole, which is shorter than its diff:
```python
import functools

import jax
import jax.numpy as jnp
from jax import lax
from jax.experimental import pallas as pl
from jax.experimental.pallas import tpu as pltpu
from jax.sharding import PartitionSpec as P

ITERS = 2
CHUNKS = 1
BLOCK = 128


def start_block(start_seeds, offset, length):
    row_col = (offset + jnp.arange(length, dtype=jnp.int32))[:, None]
    seed_row = start_seeds[None, :]
    col_ids = jnp.arange(start_seeds.shape[0], dtype=jnp.int32)[None, :] + 1
    column_term = (row_col + 1) * (col_ids * col_ids % 65521) % 65521
    hashed = (
        row_col * row_col % 65521 * (seed_row % 997 + 1) + 31 * seed_row + 7 * row_col + column_term
    ) % 65521
    return hashed.astype(jnp.float32) / 65521.0 - 0.5


def dot_t(a, b, dims, precision):
    return lax.dot_general(
        a, b, (dims, ((), ())), precision=precision, preferred_element_type=jnp.float32
    )


def invert_block(block):
    size = block.shape[0]
    lane = lax.broadcasted_iota(jnp.int32, (1, size), 1)
    lanes = lax.broadcasted_iota(jnp.int32, (size, size), 1)
    rows = lax.broadcasted_iota(jnp.int32, (size, size), 0)
    state = block
    done = []
    pivots = []
    for step in range(size):
        base = step // 8 * 8
        local_row = step - base
        pivot = state[local_row : local_row + 1, step : step + 1]
        row = state[local_row : local_row + 1, :]
        column = state[:, step : step + 1]
        scaled = jnp.where(lane == step, 1.0, row) * (1.0 / pivot)
        live_rows = rows[base:, :]
        below = live_rows > step
        kept = jnp.where(lane == step, 0.0, state)
        fresh = kept - column * scaled
        if local_row == 7:
            unit = jnp.where(lane == step, 1.0, row)
            top = jnp.concatenate([state[:7, :], unit], axis=0)
            done.append(top)
            state = fresh[8:, :]
        else:
            unit = jnp.where(lane == step, 1.0, state)
            state = jnp.where(below, fresh, jnp.where(live_rows == step, unit, state))
        pivots.append(pivot)
    return jnp.concatenate(done, axis=0), pivots


def factor_kernel(gram_ref, inverse_ref, work_ref):
    size = gram_ref.shape[0]
    work_ref[...] = gram_ref[...]
    row_ids = lax.broadcasted_iota(jnp.int32, (size, size), 0)
    col_ids = lax.broadcasted_iota(jnp.int32, (size, size), 1)
    inverse_ref[...] = jnp.where(row_ids == col_ids, 1.0, 0.0)

    @pl.loop(0, size // BLOCK)
    def _(index):
        start = pl.multiple_of(index * BLOCK, BLOCK)
        span = pl.ds(start, BLOCK)
        eliminated, pivots = invert_block(work_ref[span, span])
        block_rows = lax.broadcasted_iota(jnp.int32, (BLOCK, BLOCK), 0)
        block_cols = lax.broadcasted_iota(jnp.int32, (BLOCK, BLOCK), 1)
        scale = lax.rsqrt(jnp.concatenate(pivots, axis=0))
        inverse = jnp.where(block_rows >= block_cols, eliminated * scale, 0.0)
        high = lax.Precision.HIGHEST
        panel = dot_t(work_ref[:, span], inverse, ((1,), (1,)), high)
        panel_rows = lax.broadcasted_iota(jnp.int32, (size, BLOCK), 0)
        panel = jnp.where(panel_rows >= start + BLOCK, panel, 0.0)
        own = dot_t(inverse, inverse_ref[span, :], ((1,), (0,)), high)
        inverse_ref[span, :] = own
        inverse_ref[...] -= dot_t(panel, own, ((1,), (0,)), high)
        work_ref[...] -= dot_t(panel, panel, ((1,), (1,)), high)


def factor_inverse(gram_matrix):
    shape = jax.ShapeDtypeStruct(gram_matrix.shape, jnp.float32)
    return pl.pallas_call(
        factor_kernel,
        out_shape=shape,
        in_specs=[pl.BlockSpec(memory_space=pltpu.VMEM)],
        out_specs=pl.BlockSpec(memory_space=pltpu.VMEM),
        scratch_shapes=[pltpu.VMEM(gram_matrix.shape, jnp.float32)],
        compiler_params=pltpu.CompilerParams(vmem_limit_bytes=40 * 1024 * 1024),
        name="cholesky_inverse",
    )(gram_matrix)


def gram_of(block_rows):
    return dot_t(block_rows, block_rows, ((0,), (0,)), lax.Precision.HIGHEST)


def product(matrix, block_rows):
    return dot_t(matrix, block_rows, ((1,), (0,)), lax.Precision.HIGH)


def product_back(matrix, block_rows):
    return dot_t(matrix, block_rows, ((0,), (0,)), lax.Precision.HIGH)


def normalize(block_rows, inverse):
    return dot_t(block_rows, inverse, ((1,), (1,)), lax.Precision.HIGH)


def both(products, gram_matrix, axis):
    length = products.shape[0]
    summed = lax.psum(jnp.concatenate([products, gram_matrix], axis=0), axis)
    return summed[:length], summed[length:]


def local(direct_snapshots, adjoint_snapshots, start_seeds):
    adj_count = lax.axis_size("adj")
    adj_index = lax.axis_index("adj")
    share_rows = direct_snapshots.shape[0] // adj_count
    rank = start_seeds.shape[0]
    width = adjoint_snapshots.shape[1] // CHUNKS
    gathered = []
    tiles = []
    for chunk in range(CHUNKS):
        part = lax.all_gather(
            adjoint_snapshots[:, chunk * width : (chunk + 1) * width], "adj", axis=1, tiled=True
        )
        gathered.append(part)
        tile = dot_t(part, direct_snapshots, ((0,), (0,)), None)
        tiles.append(lax.psum_scatter(tile, "dir", scatter_dimension=0, tiled=True))
    hankel_tile = jnp.concatenate(tiles, axis=0)
    right_raw = start_block(
        start_seeds, adj_index * direct_snapshots.shape[1], direct_snapshots.shape[1]
    )
    left_raw = lax.psum(product(hankel_tile, right_raw), "adj")
    for sweep in range(ITERS):
        if sweep:
            left_next, right_gram = both(
                product(hankel_tile, right_raw), gram_of(right_raw), "adj"
            )
            left_raw = normalize(left_next, factor_inverse(right_gram))
        right_next, left_gram = both(
            product_back(hankel_tile, left_raw), gram_of(left_raw), "dir"
        )
        left_inverse = factor_inverse(left_gram)
        right_raw = normalize(right_next, left_inverse)
    left_coarse = normalize(left_raw, left_inverse).astype(jnp.bfloat16)
    left_whole = lax.all_gather(
        left_coarse.reshape(CHUNKS, -1, rank), "dir", axis=1, tiled=True
    ).reshape(-1, rank)
    right_gram = lax.psum(gram_of(right_raw), "adj")
    right_coarse = normalize(right_raw, factor_inverse(right_gram)).astype(jnp.bfloat16)
    balancing_modes = lax.psum_scatter(
        jnp.dot(direct_snapshots, right_coarse, preferred_element_type=jnp.float32),
        "adj",
        scatter_dimension=0,
        tiled=True,
    )
    own_rows = jnp.concatenate(
        [
            lax.dynamic_slice_in_dim(part, adj_index * share_rows, share_rows, 0)
            for part in gathered
        ],
        axis=1,
    )
    adjoint_modes = jnp.dot(own_rows, left_whole, preferred_element_type=jnp.float32)
    return (balancing_modes, adjoint_modes)


def solution(mesh):
    placed = (P("dir", "adj"), P("dir", "adj"), P())
    return jax.shard_map(
        local,
        mesh=mesh,
        in_specs=placed,
        out_specs=(P(("dir", "adj"), None), P(("dir", "adj"), None)),
        check_vma=False,
    )
```

time: 1460 us -> 893 us (0.61)
  other arithmetic: 498 us -> 5.1 us
  Pallas kernels: 0 us -> 212 us
  waiting for transfers between devices: 712 us -> 593 us
  matrix products: 138 us -> 51.2 us
  local copies, waits for them, and re-layouts: 76.2 us -> 7.94 us
    another operation x69 -> x0, other arithmetic: 493 us -> none  [the longest x60 322 us: normalize(): factor = jnp.linalg.cholesky(gram_matrix)]
    pallas_call x0 -> x4, Pallas kernels: none -> 212 us  [factor_inverse(): pl.pallas_call(factor_kernel, out_shape=shape, in_specs=[pl.BlockSpec(mem...]
    psum x8 -> x5, waiting for transfers between devices: 456 us -> 339 us  [the longest x3 215 us: both(): summed = lax.psum(jnp.concatenate([products, gram_matrix], axis=0), axis)]
    another operation x52 -> x0, matrix products: 69.1 us -> none  [the longest x28 41.8 us: normalize(): lax.linalg.triangular_solve(factor, raw_block, left_side=False, lower=Tru...]
    another operation x69 -> x0, local copies, waits for them, and re-layouts: 58.8 us -> none  [the longest x53 56.3 us: normalize(): lax.linalg.triangular_solve(factor, raw_block, left_side=False, lower=Tru...]
    dot_general x9 -> x14, matrix products: 61.7 us -> 45.2 us  [dot_t(): lax.dot_general(a, b, (dims, ((), ())), precision=precision, preferred_el...]
  transfers between devices with their start and end apart: 12 -> 9, of which waited for: 12 -> 9; matrix products, arithmetic and copies ran while one was open for 0% -> 1% of each run, Pallas kernels for 0% -> 0%
where the time goes in v1:
time: 893 us; the launch traced here: 885 us
  waiting for transfers between devices  593 us (66%)
  Pallas kernels  212 us (24%)
  matrix products  51.2 us (6%)
  between operations  14.5 us (2%)
    psum x3, waiting for transfers between devices, both(): summed = lax.psum(jnp.concatenate([products, gram_matrix], axis=0), axis)  215 us
    pallas_call x4, Pallas kernels, factor_inverse(): pl.pallas_call(factor_kernel, out_shape=shape, in_specs=[pl.BlockSpec(mem...  212 us
    all_gather x1, waiting for transfers between devices, local(): lax.all_gather(adjoint_snapshots[:, chunk * width:(chunk + 1) * width], '...  86.4 us
    reduce_scatter x1, waiting for transfers between devices, local(): tiles.append(lax.psum_scatter(tile, 'dir', scatter_dimension=0, tiled=True))  84.4 us
    psum x1, waiting for transfers between devices, local(): left_raw = lax.psum(product(hankel_tile, right_raw), 'adj')  65 us
    psum x1, waiting for transfers between devices, local(): right_gram = lax.psum(gram_of(right_raw), 'adj')  58.9 us
    all_gather x1, waiting for transfers between devices, local(): lax.all_gather(left_coarse.reshape(CHUNKS, -1, rank), 'dir', axis=1, tile...  51.7 us
    dot_general x14, matrix products, dot_t(): lax.dot_general(a, b, (dims, ((), ())), precision=precision, preferred_el...  45.2 us
  transfers between devices with their start and end apart: 9, of which 9 were waited for; matrix products, arithmetic and copies ran while one was open for 1% of the time, Pallas kernels for 0%

profile of v1, /device:TPU:0, one launch (start us, length us, event | category | flops | bytes accessed | tf_op | source)
XLA Modules:
  0.0 884.6 jit_solution(11019029541441869091)
XLA Ops:
  8.0 86.4 %all-gather.4.cloned.1.call-done = bf16[1024,4096]{1,0:T(8,128)(2,1)} async-done(((bf16[1024,512]{1,0:T(8,128)(2,1)}), bf16[1024,4096]{1,0:T(8,128)(2,1)}) %all-gather.4.cloned.1.call-update) | async-done | bytes 8388624 | tf_op jit(solution)/shard_map/all_gather | solution.py:133
  94.4 10.3 %fusion.46 = f32[4096,512]{1,0:T(8,128)} fusion(bf16[1024,4096]{1,0:T(8,128)(2,1)} %all-gather.4.cloned.1.call-done, bf16[1024,512]{1,0:T(8,128)(2,1)S(1)} %copy-done), kind=kOutput, calls=%fused_computation.60 | convolution fusion | flops 4294967296 | bytes 17825792 | tf_op jit(solution)/shard_map/dot_general | solution.py:27
  105.4 84.4 %reduce-scatter.3.cloned.1.call-done = f32[1024,512]{1,0:T(8,128)} async-done(((f32[4096,512]{1,0:T(8,128)}), f32[1024,512]{1,0:T(8,128)}) %reduce-scatter.3.cloned.1.call-update) | async-done | bytes 2097168 | tf_op jit(solution)/shard_map/reduce_scatter | solution.py:138
  189.9 6.0 fusion.7
  196.0 65.0 %all-reduce.6.cloned.1.call-done = f32[1024,512]{1,0:T(8,128)} async-done(((f32[1024,512]{1,0:T(8,128)}), f32[1024,512]{1,0:T(8,128)}) %all-reduce.6.cloned.1.call-update) | async-done | bytes 2097168 | tf_op jit(solution)/shard_map/psum | solution.py:143
  261.0 3.6 fusion.47
  264.6 3.7 fusion.48
  268.3 1.5 pad_maximum_fusion.1
  270.1 69.2 %all-reduce.8.cloned.1.call-done = f32[1024,512]{1,0:T(8,128)} async-done(((f32[1024,512]{1,0:T(8,128)}), f32[1024,512]{1,0:T(8,128)}) %all-reduce.8.cloned.1.call-update) | async-done | bytes 2097168 | tf_op jit(solution)/shard_map/psum | solution.py:120
  339.3 1.4 slice.25.gram_ref
  340.7 52.8 %cholesky_inverse.4 = f32[512,512]{1,0:T(8,128)S(1)} custom-call(f32[512,512]{1,0:T(8,128)S(1)} %slice.25.gram_ref), custom_call_target="tpu_custom_call" | custom-call | tf_op jit(solution)/shard_map/cholesky_inverse/pallas_call | solution.py:91
  394.5 1.9 fusion.50
  396.5 1.8 fusion.49
  398.3 2.0 pad_maximum_fusion
  400.8 76.6 %all-reduce.10.cloned.1.call-done = f32[1536,512]{1,0:T(8,128)} async-done(((f32[1536,512]{1,0:T(8,128)}), f32[1536,512]{1,0:T(8,128)}) %all-reduce.10.cloned.1.call-update) | async-done | bytes 3145744 | tf_op jit(solution)/shard_map/psum | solution.py:120
  477.5 1.4 slice.27.gram_ref
  478.9 52.9 %cholesky_inverse.5 = f32[512,512]{1,0:T(8,128)S(1)} custom-call(f32[512,512]{1,0:T(8,128)S(1)} %slice.27.gram_ref), custom_call_target="tpu_custom_call" | custom-call | tf_op jit(solution)/shard_map/cholesky_inverse/pallas_call | solution.py:91
  531.9 1.8 fusion
  533.7 3.7 fusion.52
  537.4 1.9 fusion.51
  539.3 1.5 pad_maximum_fusion.2
  540.9 69.6 %all-reduce.12.cloned.1.call-done = f32[1024,512]{1,0:T(8,128)} async-done(((f32[1024,512]{1,0:T(8,128)}), f32[1024,512]{1,0:T(8,128)}) %all-reduce.12.cloned.1.call-update) | async-done | bytes 2097168 | tf_op jit(solution)/shard_map/psum | solution.py:120
  612.0 53.0 %cholesky_inverse.6 = f32[512,512]{1,0:T(8,128)S(1)} custom-call(f32[512,512]{1,0:T(8,128)S(1)} %slice.29.gram_ref), custom_call_target="tpu_custom_call" | custom-call | tf_op jit(solution)/shard_map/cholesky_inverse/pallas_call | solution.py:91
  666.0 2.9 fusion.53
  668.9 58.9 %all-reduce.14.cloned.1.call-done.gram_ref = f32[512,512]{1,0:T(8,128)} async-done(((f32[512,512]{1,0:T(8,128)}), f32[512,512]{1,0:T(8,128)}) %all-reduce.14.cloned.1.call-update) | async-done | bytes 1048592 | tf_op jit(solution)/shard_map/psum | solution.py:159
  729.1 53.0 %cholesky_inverse.7 = f32[512,512]{1,0:T(8,128)S(1)} custom-call(f32[512,512]{1,0:T(8,128)S(1)} %copy-done.1), custom_call_target="tpu_custom_call" | custom-call | tf_op jit(solution)/shard_map/cholesky_inverse/pallas_call | solution.py:91
  783.1 2.1 convolution_bitcast_fusion
  785.3 4.4 convolution_convert_fusion
  789.8 30.4 %reduce-scatter.5.cloned.1.call-done = f32[128,512]{0,1:T(8,128)} async-done(((f32[1024,512]{0,1:T(8,128)}), f32[128,512]{0,1:T(8,128)}) %reduce-scatter.5.cloned.1.call-update) | async-done | bytes 262160 | tf_op jit(solution)/shard_map/reduce_scatter | solution.py:161
  820.1 1.8 copy.5
  821.9 51.7 %all-gather.6.cloned.1.call-done = bf16[4096,512]{1,0:T(8,128)(2,1)} async-done(((bf16[1024,512]{1,0:T(8,128)(2,1)}), bf16[4096,512]{1,0:T(8,128)(2,1)}) %all-gather.6.cloned.1.call-update) | async-done | bytes 4194320 | tf_op jit(solution)/shard_map/all_gather | solution.py:156
  873.7 3.9 fusion.13
  (43 shorter events, 8.2 us)
Async XLA Ops:
  7.2 87.2 %copy-start = (bf16[1024,512]{1,0:T(8,128)(2,1)S(1)}, bf16[1024,512]{1,0:T(8,128)(2,1)}, u32[]{:S(2)}) copy-start(bf16[1024,512]{1,0:T(8,128)(2,1)} %param.3) | copy-start | bytes 3145732
  7.2 87.2 %all-gather.4.cloned.1.call-start = ((), (), s32[]{:S(2)}) async-start(), calls=%async_computation.2 | async-start | bytes 9437184 | tf_op jit(solution)/shard_map/all_gather | solution.py:133
  7.9 182.0 %reduce-scatter.3.cloned.1.call-start = ((), (), s32[]{:S(2)}) async-start(), calls=%async_computation.3 | async-start | bytes 10485760 | tf_op jit(solution)/shard_map/reduce_scatter | solution.py:138
  104.8 0.7 copy-start.8
  104.8 156.2 %all-reduce.6.cloned.1.call-start = ((), (), s32[]{:S(2)}) async-start(), calls=%async_computation.4 | async-start | bytes 4194304 | tf_op jit(solution)/shard_map/psum | solution.py:143
  195.9 65.1 %copy-start.4 = (f32[1024,512]{1,0:T(8,128)S(1)}, f32[1024,512]{1,0:T(8,128)}, u32[]{:S(2)}) copy-start(f32[1024,512]{1,0:T(8,128)} %reduce-scatter.3.cloned.1.call-done) | copy-start | bytes 6291460
  195.9 143.3 %all-reduce.8.cloned.1.call-start = ((), (), s32[]{:S(2)}) async-start(), calls=%async_computation.5 | async-start | bytes 4194304 | tf_op jit(solution)/shard_map/psum | solution.py:120
  261.0 3.6 copy-start.3
  269.8 207.7 %all-reduce.10.cloned.1.call-start = ((), (), s32[]{:S(2)}) async-start(), calls=%async_computation.6 | async-start | bytes 6291456 | tf_op jit(solution)/shard_map/psum | solution.py:120
  339.3 54.2 %copy-start.6 = (f32[1024,512]{1,0:T(8,128)S(1)}, f32[1024,512]{1,0:T(8,128)}, u32[]{:S(2)}) copy-start(f32[1024,512]{1,0:T(8,128)} %all-reduce.8.cloned.1.call-done) | copy-start | bytes 6291460
  400.4 210.2 %all-reduce.12.cloned.1.call-start = ((), (), s32[]{:S(2)}) async-start(), calls=%async_computation.7 | async-start | bytes 4194304 | tf_op jit(solution)/shard_map/psum | solution.py:120
  477.5 54.4 %copy-start.5 = (f32[1536,512]{1,0:T(8,128)S(1)}, f32[1536,512]{1,0:T(8,128)}, u32[]{:S(2)}) copy-start(f32[1536,512]{1,0:T(8,128)} %all-reduce.10.cloned.1.call-done) | copy-start | bytes 9437188
  533.7 3.7 copy-start.2
  540.9 187.0 %all-reduce.14.cloned.1.call-start = ((), (), s32[]{:S(2)}) async-start(), calls=%async_computation.8 | async-start | bytes 2097152 | tf_op jit(solution)/shard_map/psum | solution.py:159
  610.5 54.4 %copy-start.7 = (f32[1024,512]{1,0:T(8,128)S(1)}, f32[1024,512]{1,0:T(8,128)}, u32[]{:S(2)}) copy-start(f32[1024,512]{1,0:T(8,128)} %all-reduce.12.cloned.1.call-done) | copy-start | bytes 6291460
  668.9 151.3 %reduce-scatter.5.cloned.1.call-start = ((), (), s32[]{:S(2)}) async-start(), calls=%async_computation.9 | async-start | bytes 2359296 | tf_op jit(solution)/shard_map/reduce_scatter | solution.py:161
  727.8 1.2 copy-start.1
  785.3 88.4 %all-gather.6.cloned.1.call-start = ((), (), s32[]{:S(2)}) async-start(), calls=%async_computation.10 | async-start | bytes 5242880 | tf_op jit(solution)/shard_map/all_gather | solution.py:156
Sparse Core Ops, SparseCore 0:
  9.6 84.7 all-gather.3
  104.9 84.9 reduce-scatter.2
  196.1 64.9 all-reduce.5
  269.9 69.2 all-reduce.7
  400.5 76.9 all-reduce.9
  541.0 69.4 all-reduce.11
  669.0 58.8 all-reduce.13
  785.4 34.7 reduce-scatter.4
  822.1 51.4 all-gather.5

commit v2 on v1

--- a/solution.py
+++ b/solution.py
@@ -1,5 +1,3 @@
-import functools
-
 import jax
 import jax.numpy as jnp
 from jax import lax
@@ -8,7 +6,6 @@
 from jax.sharding import PartitionSpec as P
 
 ITERS = 2
-CHUNKS = 1
 BLOCK = 128
 
 
@@ -116,27 +113,19 @@
 
 
 def both(products, gram_matrix, axis):
-    length = products.shape[0]
-    summed = lax.psum(jnp.concatenate([products, gram_matrix], axis=0), axis)
-    return summed[:length], summed[length:]
+    gram_sum, products = lax.optimization_barrier((lax.psum(gram_matrix, axis), products))
+    return lax.psum(products, axis), gram_sum
 
 
 def local(direct_snapshots, adjoint_snapshots, start_seeds):
     adj_count = lax.axis_size("adj")
     adj_index = lax.axis_index("adj")
     share_rows = direct_snapshots.shape[0] // adj_count
-    rank = start_seeds.shape[0]
-    width = adjoint_snapshots.shape[1] // CHUNKS
-    gathered = []
-    tiles = []
-    for chunk in range(CHUNKS):
-        part = lax.all_gather(
-            adjoint_snapshots[:, chunk * width : (chunk + 1) * width], "adj", axis=1, tiled=True
-        )
-        gathered.append(part)
-        tile = dot_t(part, direct_snapshots, ((0,), (0,)), None)
-        tiles.append(lax.psum_scatter(tile, "dir", scatter_dimension=0, tiled=True))
-    hankel_tile = jnp.concatenate(tiles, axis=0)
+    dir_count = lax.axis_size("dir")
+    turned = lax.all_to_all(adjoint_snapshots, "dir", split_axis=1, concat_axis=0, tiled=True)
+    gathered = lax.all_gather(turned, "adj", axis=1, tiled=True)
+    direct_whole = lax.all_gather(direct_snapshots, "dir", axis=0, tiled=True)
+    hankel_tile = dot_t(gathered, direct_whole, ((0,), (0,)), None)
     right_raw = start_block(
         start_seeds, adj_index * direct_snapshots.shape[1], direct_snapshots.shape[1]
     )
@@ -153,25 +142,29 @@
         left_inverse = factor_inverse(left_gram)
         right_raw = normalize(right_next, left_inverse)
     left_coarse = normalize(left_raw, left_inverse).astype(jnp.bfloat16)
-    left_whole = lax.all_gather(
-        left_coarse.reshape(CHUNKS, -1, rank), "dir", axis=1, tiled=True
-    ).reshape(-1, rank)
     right_gram = lax.psum(gram_of(right_raw), "adj")
-    right_coarse = normalize(right_raw, factor_inverse(right_gram)).astype(jnp.bfloat16)
+    right_gram, left_coarse = lax.optimization_barrier((right_gram, left_coarse))
+    own_states = lax.dynamic_index_in_dim(
+        gathered.reshape(dir_count, adj_count, share_rows, -1), adj_index, 1, keepdims=False
+    )
+    adjoint_modes = lax.psum_scatter(
+        jnp.dot(
+            own_states.reshape(dir_count * share_rows, -1),
+            left_coarse,
+            preferred_element_type=jnp.float32,
+        ),
+        "dir",
+        scatter_dimension=0,
+        tiled=True,
+    )
+    right_inverse, adjoint_modes = lax.optimization_barrier((factor_inverse(right_gram), adjoint_modes))
+    right_coarse = normalize(right_raw, right_inverse).astype(jnp.bfloat16)
     balancing_modes = lax.psum_scatter(
         jnp.dot(direct_snapshots, right_coarse, preferred_element_type=jnp.float32),
         "adj",
         scatter_dimension=0,
         tiled=True,
     )
-    own_rows = jnp.concatenate(
-        [
-            lax.dynamic_slice_in_dim(part, adj_index * share_rows, share_rows, 0)
-            for part in gathered
-        ],
-        axis=1,
-    )
-    adjoint_modes = jnp.dot(own_rows, left_whole, preferred_element_type=jnp.float32)
     return (balancing_modes, adjoint_modes)
 
 

time: 893 us -> 773 us (0.87)
  waiting for transfers between devices: 593 us -> 439 us
  blocking collectives: 0 us -> 24.8 us
    reduce_scatter x1, waiting for transfers between devices: 84.4 us -> 0.02 us  [local(): lax.psum_scatter(jnp.dot(own_states.reshape(dir_count * share_rows, -1),...]
    psum x3 -> x6, waiting for transfers between devices: 215 us -> 169 us  [the longest x3 151 us: both(): lax.psum(gram_matrix, axis)]
    all_to_all x0 -> x1, blocking collectives: none -> 24.8 us  [local(): lax.all_to_all(adjoint_snapshots, 'dir', split_axis=1, concat_axis=0, til...]
    all_gather x2, waiting for transfers between devices: 138 us -> 118 us  [the longest x1 84.1 us: local(): gathered = lax.all_gather(turned, 'adj', axis=1, tiled=True)]
  transfers between devices with their start and end apart: 9 -> 12, of which waited for: 9 -> 11; matrix products, arithmetic and copies ran while one was open for 1% -> 3% of each run, Pallas kernels for 0% -> 28%
where the time goes in v2:
time: 773 us; the launch traced here: 765 us
  waiting for transfers between devices  439 us (57%)
  Pallas kernels  211 us (27%)
  matrix products  60.1 us (8%)
  blocking collectives  24.8 us (3%)
  between operations  14.8 us (2%)
  local copies, waits for them, and re-layouts  12.8 us (2%)
    pallas_call x4, Pallas kernels, factor_inverse(): pl.pallas_call(factor_kernel, out_shape=shape, in_specs=[pl.BlockSpec(mem...  211 us
    psum x3, waiting for transfers between devices, both(): lax.psum(gram_matrix, axis)  151 us
    all_gather x1, waiting for transfers between devices, local(): gathered = lax.all_gather(turned, 'adj', axis=1, tiled=True)  84.1 us
    psum x1, waiting for transfers between devices, local(): left_raw = lax.psum(product(hankel_tile, right_raw), 'adj')  63.1 us
    psum x1, waiting for transfers between devices, local(): right_gram = lax.psum(gram_of(right_raw), 'adj')  53.6 us
    dot_general x14, matrix products, dot_t(): lax.dot_general(a, b, (dims, ((), ())), precision=precision, preferred_el...  53.5 us
    reduce_scatter x1, waiting for transfers between devices, local(): lax.psum_scatter(jnp.dot(direct_snapshots, right_coarse, preferred_elemen...  34.9 us
    all_gather x1, waiting for transfers between devices, local(): direct_whole = lax.all_gather(direct_snapshots, 'dir', axis=0, tiled=True)  34.2 us
  transfers between devices with their start and end apart: 12, of which 11 were waited for; matrix products, arithmetic and copies ran while one was open for 3% of the time, Pallas kernels for 28%

profile of v2, /device:TPU:0, one launch (start us, length us, event | category | flops | bytes accessed | tf_op | source)
XLA Modules:
  0.0 764.6 jit_solution(16409110064230719312)
XLA Ops:
  9.4 24.8 %all_to_all.19 = bf16[1024,4,128]{0,2,1:T(8,128)(2,1)S(1)} all-to-all(bf16[1024,4,128]{0,2,1:T(8,128)(2,1)S(1)} %bitcast.40), channel_id=1, replica_groups=mesh['dir'=4,'adj'=8] {'dir'}, dimensions={1} | all-to-all | bytes 2097152 | tf_op jit(solution)/shard_map/all_to_all | solution.py:125
  35.7 34.2 %all-gather.5.cloned.1.call-done = bf16[4096,512]{1,0:T(8,128)(2,1)} async-done(((bf16[1024,512]{1,0:T(8,128)(2,1)}), bf16[4096,512]{1,0:T(8,128)(2,1)}) %all-gather.5.cloned.1.call-update) | async-done | bytes 4194320 | tf_op jit(solution)/shard_map/all_gather | solution.py:127
  70.0 84.1 %all-gather.3.cloned.1.call-done = bf16[4096,1024]{1,0:T(8,128)(2,1)} async-done(((bf16[4096,128]{1,0:T(8,128)(2,1)}), bf16[4096,1024]{1,0:T(8,128)(2,1)}) %all-gather.3.cloned.1.call-update) | async-done | bytes 8388624 | tf_op jit(solution)/shard_map/all_gather | solution.py:126
  154.1 8.2 %fusion.37 = f32[1024,512]{1,0:T(8,128)S(1)} fusion(bf16[4096,1024]{1,0:T(8,128)(2,1)} %all-gather.3.cloned.1.call-done, bf16[4096,512]{1,0:T(8,128)(2,1)} %all-gather.5.cloned.1.call-done), kind=kOutput, calls=%fused_computation.49 | convolution fusion | flops 4294967296 | bytes 14680064 | tf_op jit(solution)/shard_map/dot_general | solution.py:24
  163.7 4.5 fusion.5
  168.2 63.1 %all-reduce.9.cloned.1.call-done = f32[1024,512]{1,0:T(8,128)} async-done(((f32[1024,512]{1,0:T(8,128)}), f32[1024,512]{1,0:T(8,128)}) %all-reduce.9.cloned.1.call-update) | async-done | bytes 2097168 | tf_op jit(solution)/shard_map/psum | solution.py:132
  231.3 6.8 fusion.38
  238.3 4.4 fusion.39
  242.7 47.9 %all-reduce.11.cloned.1.call-done.gram_ref = f32[512,512]{1,0:T(8,128)} async-done(((f32[512,512]{1,0:T(8,128)}), f32[512,512]{1,0:T(8,128)}) %all-reduce.11.cloned.1.call-update) | async-done | bytes 1048592 | tf_op jit(solution)/shard_map/psum | solution.py:116
  292.3 52.8 %cholesky_inverse.4 = f32[512,512]{1,0:T(8,128)S(1)} custom-call(f32[512,512]{1,0:T(8,128)S(1)} %copy-done.1), custom_call_target="tpu_custom_call" | custom-call | tf_op jit(solution)/shard_map/cholesky_inverse/pallas_call | solution.py:88
  345.1 2.0 all-reduce.13.cloned.1.call-done
  347.0 2.3 fusion.40
  349.3 2.9 fusion.41
  352.3 3.1 fusion.42
  355.4 55.8 %all-reduce.15.cloned.1.call-done.gram_ref = f32[512,512]{1,0:T(8,128)} async-done(((f32[512,512]{1,0:T(8,128)}), f32[512,512]{1,0:T(8,128)}) %all-reduce.15.cloned.1.call-update) | async-done | bytes 1048592 | tf_op jit(solution)/shard_map/psum | solution.py:116
  412.5 52.8 %cholesky_inverse.5 = f32[512,512]{1,0:T(8,128)S(1)} custom-call(f32[512,512]{1,0:T(8,128)S(1)} %copy-done.2), custom_call_target="tpu_custom_call" | custom-call | tf_op jit(solution)/shard_map/cholesky_inverse/pallas_call | solution.py:88
  465.2 12.8 %all-reduce.17.cloned.1.call-done = f32[1024,512]{1,0:T(8,128)} async-done(((f32[1024,512]{1,0:T(8,128)}), f32[1024,512]{1,0:T(8,128)}) %all-reduce.17.cloned.1.call-update) | async-done | bytes 2097168 | tf_op jit(solution)/shard_map/psum | solution.py:117
  478.1 3.4 fusion.43
  481.5 4.6 fusion.44
  486.3 4.4 fusion.45
  490.8 47.6 %all-reduce.19.cloned.1.call-done.gram_ref = f32[512,512]{1,0:T(8,128)} async-done(((f32[512,512]{1,0:T(8,128)}), f32[512,512]{1,0:T(8,128)}) %all-reduce.19.cloned.1.call-update) | async-done | bytes 1048592 | tf_op jit(solution)/shard_map/psum | solution.py:116
  539.7 52.8 %cholesky_inverse.6 = f32[512,512]{1,0:T(8,128)S(1)} custom-call(f32[512,512]{1,0:T(8,128)S(1)} %copy-done.3), custom_call_target="tpu_custom_call" | custom-call | tf_op jit(solution)/shard_map/cholesky_inverse/pallas_call | solution.py:88
  592.4 2.5 all-reduce.21.cloned.1.call-done
  594.9 2.3 fusion.46
  598.2 2.8 fusion.47
  601.4 2.3 constant_dynamic-slice_fusion
  603.7 2.8 convolution_convert_fusion
  606.5 53.6 %all-reduce.23.cloned.1.call-done.gram_ref = f32[512,512]{1,0:T(8,128)} async-done(((f32[512,512]{1,0:T(8,128)}), f32[512,512]{1,0:T(8,128)}) %all-reduce.23.cloned.1.call-update) | async-done | bytes 1048592 | tf_op jit(solution)/shard_map/psum | solution.py:145
  660.1 3.3 fusion.48
  663.5 52.8 %cholesky_inverse.7 = f32[512,512]{1,0:T(8,128)S(1)} custom-call(f32[512,512]{1,0:T(8,128)S(1)} %copy-done), custom_call_target="tpu_custom_call" | custom-call | tf_op jit(solution)/shard_map/cholesky_inverse/pallas_call | solution.py:88
  717.3 3.3 convolution_bitcast_fusion
  720.7 34.9 %reduce-scatter.5.cloned.1.call-done = f32[128,512]{0,1:T(8,128)} async-done(((f32[1024,512]{0,1:T(8,128)}), f32[128,512]{0,1:T(8,128)}) %reduce-scatter.5.cloned.1.call-update) | async-done | bytes 262160 | tf_op jit(solution)/shard_map/reduce_scatter | solution.py:162
  (52 shorter events, 14.0 us)
Async XLA Ops:
  7.2 62.8 %all-gather.5.cloned.1.call-start = ((), (), s32[]{:S(2)}) async-start(), calls=%async_computation.4 | async-start | bytes 5242880 | tf_op jit(solution)/shard_map/all_gather | solution.py:127
  7.9 146.2 %all-gather.3.cloned.1.call-start = ((), (), s32[]{:S(2)}) async-start(), calls=%async_computation.3 | async-start | bytes 9437184 | tf_op jit(solution)/shard_map/all_gather | solution.py:126
  34.3 1.4 copy-start.9
  35.6 195.7 %all-reduce.9.cloned.1.call-start = ((), (), s32[]{:S(2)}) async-start(), calls=%async_computation.5 | async-start | bytes 4194304 | tf_op jit(solution)/shard_map/psum | solution.py:132
  162.3 1.4 copy-start.5
  168.2 122.4 %all-reduce.11.cloned.1.call-start = ((), (), s32[]{:S(2)}) async-start(), calls=%async_computation.6 | async-start | bytes 2097152 | tf_op jit(solution)/shard_map/psum | solution.py:116
  231.3 6.9 copy-start.4
  238.2 108.8 %all-reduce.13.cloned.1.call-start = ((), (), s32[]{:S(2)}) async-start(), calls=%async_computation.7 | async-start | bytes 2097152 | tf_op jit(solution)/shard_map/psum | solution.py:117
  290.6 120.7 %all-reduce.15.cloned.1.call-start = ((), (), s32[]{:S(2)}) async-start(), calls=%async_computation.8 | async-start | bytes 2097152 | tf_op jit(solution)/shard_map/psum | solution.py:116
  291.1 1.2 copy-start.1
  349.3 3.0 copy-start.6
  352.2 125.9 %all-reduce.17.cloned.1.call-start = ((), (), s32[]{:S(2)}) async-start(), calls=%async_computation.9 | async-start | bytes 4194304 | tf_op jit(solution)/shard_map/psum | solution.py:117
  411.2 1.2 copy-start.2
  411.3 127.1 %all-reduce.19.cloned.1.call-start = ((), (), s32[]{:S(2)}) async-start(), calls=%async_computation.10 | async-start | bytes 2097152 | tf_op jit(solution)/shard_map/psum | solution.py:116
  486.1 108.8 %all-reduce.21.cloned.1.call-start = ((), (), s32[]{:S(2)}) async-start(), calls=%async_computation.11 | async-start | bytes 2097152 | tf_op jit(solution)/shard_map/psum | solution.py:117
  538.4 121.7 %all-reduce.23.cloned.1.call-start = ((), (), s32[]{:S(2)}) async-start(), calls=%async_computation.12 | async-start | bytes 2097152 | tf_op jit(solution)/shard_map/psum | solution.py:145
  538.4 1.2 copy-start.3
  597.2 1.0 copy-start.7
  601.1 115.2 %reduce-scatter.3.cloned.1.call-start = ((), (), s32[]{:S(2)}) async-start(), calls=%async_computation.13 | async-start | bytes 1310720 | tf_op jit(solution)/shard_map/reduce_scatter | solution.py:150
  660.1 3.4 copy-start
  663.4 52.9 %copy-start.8 = (f32[512,512]{1,0:T(8,128)S(1)}, f32[512,512]{1,0:T(8,128)}, u32[]{:S(2)}) copy-start(f32[512,512]{1,0:T(8,128)} %copy-done.7) | copy-start | bytes 3145732
  663.4 92.1 %reduce-scatter.5.cloned.1.call-start = ((), (), s32[]{:S(2)}) async-start(), calls=%async_computation.14 | async-start | bytes 2359296 | tf_op jit(solution)/shard_map/reduce_scatter | solution.py:162
Sparse Core Ops, SparseCore 0:
  9.8 60.0 all-gather.4
  71.6 82.4 all-gather.2
  168.3 63.0 all-reduce.8
  238.3 52.1 all-reduce.10
  293.5 53.5 all-reduce.12
  352.3 58.8 all-reduce.14
  413.6 64.4 all-reduce.16
  486.2 52.1 all-reduce.18
  541.4 53.4 all-reduce.20
  601.2 58.8 all-reduce.22
  663.5 26.7 reduce-scatter.2
  720.8 34.7 reduce-scatter.4

commit v3 on v2

--- a/solution.py
+++ b/solution.py
@@ -1,3 +1,5 @@
+import functools
+
 import jax
 import jax.numpy as jnp
 from jax import lax
@@ -112,8 +114,93 @@
     return dot_t(block_rows, inverse, ((1,), (1,)), lax.Precision.HIGH)
 
 
+def sum_kernel(axis, pair, count, x_ref, out_ref, held, work, landed, send_sem, recv_sem):
+    dir_index, adj_index = lax.axis_index("dir"), lax.axis_index("adj")
+    me = dir_index if axis == "dir" else adj_index
+    chips = count // pair
+    core, chip = lax.rem(me, pair), me // pair
+    length = x_ref.shape[0] // pair
+    part = length // chips
+
+    def device(index):
+        return (index, adj_index) if axis == "dir" else (dir_index, index)
+
+    others = [lax.rem(chip + away, chips) * pair + core for away in range(1, chips)]
+    partner = chip * pair + (1 - core)
+    peers = others + ([partner] if pair == 2 else [])
+    barrier = pltpu.get_barrier_semaphore()
+    for peer in peers:
+        pl.semaphore_signal(
+            barrier, inc=1, device_id=device(peer), device_id_type=pl.DeviceIdType.MESH
+        )
+    pl.semaphore_wait(barrier, len(peers))
+
+    def send(source, target, slot, peer):
+        copy = pltpu.make_async_remote_copy(
+            src_ref=source,
+            dst_ref=target,
+            send_sem=send_sem.at[slot],
+            recv_sem=recv_sem.at[slot],
+            device_id=device(peer),
+            device_id_type=pl.DeviceIdType.MESH,
+        )
+        copy.start()
+        return copy
+
+    own_half = pl.ds(pl.multiple_of(core * length, 8), length)
+    if pair == 2:
+        other_half = pl.ds(pl.multiple_of((1 - core) * length, 8), length)
+        send(x_ref.at[other_half], held, 0, partner).wait()
+        work[...] = x_ref[own_half, :] + held[...]
+    else:
+        work[...] = x_ref[...]
+    copies = []
+    for away, peer in enumerate(others, 1):
+        rows = pl.ds(pl.multiple_of(lax.rem(chip + away, chips) * part, 8), part)
+        copies.append(send(work.at[rows], landed.at[away - 1], away, peer))
+    total = work[pl.ds(pl.multiple_of(chip * part, 8), part), :]
+    for away, copy in enumerate(copies):
+        copy.wait()
+        total = total + landed[away]
+    own_part = pl.ds(pl.multiple_of(core * length + chip * part, 8), part)
+    out_ref[own_part, :] = total
+    copies = [
+        send(out_ref.at[own_part], out_ref.at[own_part], chips + away, peer)
+        for away, peer in enumerate(others)
+    ]
+    for copy in copies:
+        copy.wait()
+    if pair == 2:
+        send(out_ref.at[own_half], out_ref.at[own_half], 2 * chips, partner).wait()
+
+
+def sum_over(value, axis):
+    count = lax.axis_size(axis)
+    pair = 2 if axis == "adj" else 1
+    rows, columns = value.shape
+    chips = count // pair
+    held_rows = rows // pair if pair == 2 else 8
+    return pl.pallas_call(
+        functools.partial(sum_kernel, axis, pair, count),
+        out_shape=jax.ShapeDtypeStruct(value.shape, jnp.float32),
+        in_specs=[pl.BlockSpec(memory_space=pltpu.VMEM)],
+        out_specs=pl.BlockSpec(memory_space=pltpu.VMEM),
+        scratch_shapes=[
+            pltpu.VMEM((held_rows, columns), jnp.float32),
+            pltpu.VMEM((rows // pair, columns), jnp.float32),
+            pltpu.VMEM((chips - 1, rows // pair // chips, columns), jnp.float32),
+            pltpu.SemaphoreType.DMA((2 * chips + 1,)),
+            pltpu.SemaphoreType.DMA((2 * chips + 1,)),
+        ],
+        compiler_params=pltpu.CompilerParams(
+            collective_id=1 if axis == "dir" else 2, vmem_limit_bytes=40 * 1024 * 1024
+        ),
+        name="gram_sum_" + axis,
+    )(value)
+
+
 def both(products, gram_matrix, axis):
-    gram_sum, products = lax.optimization_barrier((lax.psum(gram_matrix, axis), products))
+    gram_sum, products = lax.optimization_barrier((sum_over(gram_matrix, axis), products))
     return lax.psum(products, axis), gram_sum
 
 
@@ -142,7 +229,7 @@
         left_inverse = factor_inverse(left_gram)
         right_raw = normalize(right_next, left_inverse)
     left_coarse = normalize(left_raw, left_inverse).astype(jnp.bfloat16)
-    right_gram = lax.psum(gram_of(right_raw), "adj")
+    right_gram = sum_over(gram_of(right_raw), "adj")
     right_gram, left_coarse = lax.optimization_barrier((right_gram, left_coarse))
     own_states = lax.dynamic_index_in_dim(
         gathered.reshape(dir_count, adj_count, share_rows, -1), adj_index, 1, keepdims=False

time: 773 us -> 663 us (0.86)
  waiting for transfers between devices: 439 us -> 236 us
  Pallas kernels: 211 us -> 320 us
  matrix products: 60.1 us -> 51.6 us
    psum x4 -> x0, waiting for transfers between devices: 205 us -> none  [the longest x3 151 us: both(): lax.psum(gram_matrix, axis)]
    pallas_call x0 -> x4, Pallas kernels: none -> 108 us  [sum_over(): pl.pallas_call(functools.partial(sum_kernel, axis, pair, count), out_shap...]
  transfers between devices with their start and end apart: 12 -> 8, of which waited for: 11 -> 6; matrix products, arithmetic and copies ran while one was open for 3% -> 1% of each run, Pallas kernels for 28% -> 32%
where the time goes in v3:
time: 663 us; the launch traced here: 654 us
  Pallas kernels  320 us (48%)
  waiting for transfers between devices  236 us (36%)
  matrix products  51.6 us (8%)
  blocking collectives  24.8 us (4%)
  between operations  14.8 us (2%)
    pallas_call x4, Pallas kernels, factor_inverse(): pl.pallas_call(factor_kernel, out_shape=shape, in_specs=[pl.BlockSpec(mem...  212 us
    pallas_call x4, Pallas kernels, sum_over(): pl.pallas_call(functools.partial(sum_kernel, axis, pair, count), out_shap...  108 us
    all_gather x1, waiting for transfers between devices, local(): gathered = lax.all_gather(turned, 'adj', axis=1, tiled=True)  84.1 us
    psum x1, waiting for transfers between devices, local(): left_raw = lax.psum(product(hankel_tile, right_raw), 'adj')  63.1 us
    dot_general x14, matrix products, dot_t(): lax.dot_general(a, b, (dims, ((), ())), precision=precision, preferred_el...  46.6 us
    reduce_scatter x1, waiting for transfers between devices, local(): lax.psum_scatter(jnp.dot(direct_snapshots, right_coarse, preferred_elemen...  39.3 us
    all_gather x1, waiting for transfers between devices, local(): direct_whole = lax.all_gather(direct_snapshots, 'dir', axis=0, tiled=True)  34.2 us
    all_to_all x1, blocking collectives, local(): lax.all_to_all(adjoint_snapshots, 'dir', split_axis=1, concat_axis=0, til...  24.8 us
  transfers between devices with their start and end apart: 8, of which 6 were waited for; matrix products, arithmetic and copies ran while one was open for 1% of the time, Pallas kernels for 32%

profile of v3, /device:TPU:0, one launch (start us, length us, event | category | flops | bytes accessed | tf_op | source)
XLA Modules:
  0.0 654.3 jit_solution(2054693425404858941)
XLA Ops:
  7.9 1.5 copy.7
  9.4 24.8 %all_to_all.19 = bf16[1024,4,128]{0,2,1:T(8,128)(2,1)S(1)} all-to-all(bf16[1024,4,128]{0,2,1:T(8,128)(2,1)S(1)} %bitcast.40), channel_id=1, replica_groups=mesh['dir'=4,'adj'=8] {'dir'}, dimensions={1} | all-to-all | bytes 2097152 | tf_op jit(solution)/shard_map/all_to_all | solution.py:212
  35.8 34.2 %all-gather.5.cloned.1.call-done = bf16[4096,512]{1,0:T(8,128)(2,1)} async-done(((bf16[1024,512]{1,0:T(8,128)(2,1)}), bf16[4096,512]{1,0:T(8,128)(2,1)}) %all-gather.5.cloned.1.call-update) | async-done | bytes 4194320 | tf_op jit(solution)/shard_map/all_gather | solution.py:214
  70.0 84.1 %all-gather.3.cloned.1.call-done = bf16[4096,1024]{1,0:T(8,128)(2,1)} async-done(((bf16[4096,128]{1,0:T(8,128)(2,1)}), bf16[4096,1024]{1,0:T(8,128)(2,1)}) %all-gather.3.cloned.1.call-update) | async-done | bytes 8388624 | tf_op jit(solution)/shard_map/all_gather | solution.py:213
  154.1 8.2 %fusion.37 = f32[1024,512]{1,0:T(8,128)S(1)} fusion(bf16[4096,1024]{1,0:T(8,128)(2,1)} %all-gather.3.cloned.1.call-done, bf16[4096,512]{1,0:T(8,128)(2,1)} %all-gather.5.cloned.1.call-done), kind=kOutput, calls=%fused_computation.49 | convolution fusion | flops 4294967296 | bytes 14680064 | tf_op jit(solution)/shard_map/dot_general | solution.py:26
  162.3 4.5 fusion.5
  166.8 63.1 %all-reduce.5.cloned.1.call-done = f32[1024,512]{1,0:T(8,128)} async-done(((f32[1024,512]{1,0:T(8,128)}), f32[1024,512]{1,0:T(8,128)}) %all-reduce.5.cloned.1.call-update) | async-done | bytes 2097168 | tf_op jit(solution)/shard_map/psum | solution.py:219
  230.0 5.7 fusion.38.x_ref
  235.7 25.4 %gram_sum_dir.2.gram_ref = f32[512,512]{1,0:T(8,128)S(1)} custom-call(f32[512,512]{1,0:T(8,128)S(1)} %fusion.38.x_ref), custom_call_target="tpu_custom_call" | custom-call | tf_op jit(solution)/shard_map/gram_sum_dir/pallas_call | solution.py:183
  261.1 2.8 fusion.39
  264.3 52.8 %cholesky_inverse.4 = f32[512,512]{1,0:T(8,128)S(1)} custom-call(f32[512,512]{1,0:T(8,128)S(1)} %gram_sum_dir.2.gram_ref), custom_call_target="tpu_custom_call" | custom-call | tf_op jit(solution)/shard_map/cholesky_inverse/pallas_call | solution.py:90
  317.3 2.3 fusion.40
  319.6 1.9 fusion.41.x_ref
  321.5 3.2 fusion.42
  324.7 29.0 %gram_sum_adj.2.gram_ref = f32[512,512]{1,0:T(8,128)S(1)} custom-call(f32[512,512]{1,0:T(8,128)S(1)} %fusion.41.x_ref), custom_call_target="tpu_custom_call" | custom-call | tf_op jit(solution)/shard_map/gram_sum_adj/pallas_call | solution.py:183
  354.4 52.9 %cholesky_inverse.5 = f32[512,512]{1,0:T(8,128)S(1)} custom-call(f32[512,512]{1,0:T(8,128)S(1)} %gram_sum_adj.2.gram_ref), custom_call_target="tpu_custom_call" | custom-call | tf_op jit(solution)/shard_map/cholesky_inverse/pallas_call | solution.py:90
  407.3 14.2 %all-reduce.9.cloned.1.call-done = f32[1024,512]{1,0:T(8,128)} async-done(((f32[1024,512]{1,0:T(8,128)}), f32[1024,512]{1,0:T(8,128)}) %all-reduce.9.cloned.1.call-update) | async-done | bytes 2097168 | tf_op jit(solution)/shard_map/psum | solution.py:204
  421.5 3.6 fusion.43
  425.1 2.9 fusion.45
  428.0 3.5 fusion.44.x_ref
  431.5 25.5 %gram_sum_dir.3.gram_ref = f32[512,512]{1,0:T(8,128)S(1)} custom-call(f32[512,512]{1,0:T(8,128)S(1)} %fusion.44.x_ref), custom_call_target="tpu_custom_call" | custom-call | tf_op jit(solution)/shard_map/gram_sum_dir/pallas_call | solution.py:183
  457.1 1.5 constant_dynamic-slice_fusion
  458.6 53.0 %cholesky_inverse.6 = f32[512,512]{1,0:T(8,128)S(1)} custom-call(f32[512,512]{1,0:T(8,128)S(1)} %gram_sum_dir.3.gram_ref), custom_call_target="tpu_custom_call" | custom-call | tf_op jit(solution)/shard_map/cholesky_inverse/pallas_call | solution.py:90
  511.6 2.8 convolution_convert_fusion
  514.4 2.3 fusion.46
  516.7 1.9 fusion.47.x_ref
  518.5 28.3 %gram_sum_adj.3.gram_ref = f32[512,512]{1,0:T(8,128)S(1)} custom-call(f32[512,512]{1,0:T(8,128)S(1)} %fusion.47.x_ref), custom_call_target="tpu_custom_call" | custom-call | tf_op jit(solution)/shard_map/gram_sum_adj/pallas_call | solution.py:183
  546.8 1.7 fusion.48
  548.6 53.0 %cholesky_inverse.7 = f32[512,512]{1,0:T(8,128)S(1)} custom-call(f32[512,512]{1,0:T(8,128)S(1)} %gram_sum_adj.3.gram_ref), custom_call_target="tpu_custom_call" | custom-call | tf_op jit(solution)/shard_map/cholesky_inverse/pallas_call | solution.py:90
  602.7 3.3 convolution_bitcast_fusion
  606.0 39.3 %reduce-scatter.5.cloned.1.call-done = f32[128,512]{0,1:T(8,128)} async-done(((f32[1024,512]{0,1:T(8,128)}), f32[128,512]{0,1:T(8,128)}) %reduce-scatter.5.cloned.1.call-update) | async-done | bytes 262160 | tf_op jit(solution)/shard_map/reduce_scatter | solution.py:249
  645.3 1.8 copy.9
  (40 shorter events, 4.7 us)
Async XLA Ops:
  7.2 62.8 %all-gather.5.cloned.1.call-start = ((), (), s32[]{:S(2)}) async-start(), calls=%async_computation.4 | async-start | bytes 5242880 | tf_op jit(solution)/shard_map/all_gather | solution.py:214
  7.9 146.2 %all-gather.3.cloned.1.call-start = ((), (), s32[]{:S(2)}) async-start(), calls=%async_computation.3 | async-start | bytes 9437184 | tf_op jit(solution)/shard_map/all_gather | solution.py:213
  34.3 1.4 copy-start.7
  35.6 194.3 %all-reduce.5.cloned.1.call-start = ((), (), s32[]{:S(2)}) async-start(), calls=%async_computation.5 | async-start | bytes 4194304 | tf_op jit(solution)/shard_map/psum | solution.py:219
  162.3 98.8 %copy-start.3 = (f32[1024,512]{1,0:T(8,128)}, f32[1024,512]{1,0:T(8,128)S(1)}, u32[]{:S(2)}) copy-start(f32[1024,512]{1,0:T(8,128)S(1)} %fusion.37) | copy-start | bytes 6291460
  166.8 150.5 %all-reduce.7.cloned.1.call-start = ((), (), s32[]{:S(2)}) async-start(), calls=%async_computation.6 | async-start | bytes 2097152 | tf_op jit(solution)/shard_map/psum | solution.py:204
  235.7 25.4 %copy-start.2 = (f32[1024,512]{1,0:T(8,128)S(1)}, f32[1024,512]{1,0:T(8,128)}, u32[]{:S(2)}) copy-start(f32[1024,512]{1,0:T(8,128)} %all-reduce.5.cloned.1.call-done) | copy-start | bytes 6291460
  264.0 157.5 %all-reduce.9.cloned.1.call-start = ((), (), s32[]{:S(2)}) async-start(), calls=%async_computation.7 | async-start | bytes 4194304 | tf_op jit(solution)/shard_map/psum | solution.py:204
  319.6 1.9 copy-start.4
  353.8 160.6 %all-reduce.11.cloned.1.call-start = ((), (), s32[]{:S(2)}) async-start(), calls=%async_computation.8 | async-start | bytes 2097152 | tf_op jit(solution)/shard_map/psum | solution.py:204
  421.5 3.6 copy-start.5
  425.1 3.0 copy-start
  457.1 144.5 %reduce-scatter.3.cloned.1.call-start = ((), (), s32[]{:S(2)}) async-start(), calls=%async_computation.9 | async-start | bytes 1310720 | tf_op jit(solution)/shard_map/reduce_scatter | solution.py:237
  457.1 54.4 %copy-start.1 = (f32[1024,512]{1,0:T(8,128)S(1)}, f32[1024,512]{1,0:T(8,128)}, u32[]{:S(2)}) copy-start(f32[1024,512]{1,0:T(8,128)} %copy-done) | copy-start | bytes 6291460
  516.7 30.2 %copy-start.6 = (bf16[1024,512]{1,0:T(8,128)(2,1)S(1)}, bf16[1024,512]{1,0:T(8,128)(2,1)}, u32[]{:S(2)}) copy-start(bf16[1024,512]{1,0:T(8,128)(2,1)} %convolution_convert_fusion) | copy-start | bytes 3145732
  548.5 96.7 %reduce-scatter.5.cloned.1.call-start = ((), (), s32[]{:S(2)}) async-start(), calls=%async_computation.10 | async-start | bytes 2359296 | tf_op jit(solution)/shard_map/reduce_scatter | solution.py:249
Sparse Core Ops, SparseCore 0:
  9.8 60.0 all-gather.4
  71.6 82.4 all-gather.2
  166.9 63.0 all-reduce.4
  264.1 53.1 all-reduce.6
  353.9 67.5 all-reduce.8
  457.2 52.2 all-reduce.10
  548.7 31.0 reduce-scatter.2
  606.1 39.0 reduce-scatter.4

commit v4 on v3

--- a/solution.py
+++ b/solution.py
@@ -174,6 +174,55 @@
         send(out_ref.at[own_half], out_ref.at[own_half], 2 * chips, partner).wait()
 
 
+def gather_kernel(count, x_ref, out_ref, local_sem, send_sem, recv_sem):
+    me, adj_index = lax.axis_index("dir"), lax.axis_index("adj")
+    length = x_ref.shape[0]
+    peers = [lax.rem(me + away, count) for away in range(1, count)]
+    barrier = pltpu.get_barrier_semaphore()
+    for peer in peers:
+        pl.semaphore_signal(
+            barrier, inc=1, device_id=(peer, adj_index), device_id_type=pl.DeviceIdType.MESH
+        )
+    pl.semaphore_wait(barrier, len(peers))
+    own = out_ref.at[pl.ds(pl.multiple_of(me * length, 16), length)]
+    copies = [
+        pltpu.make_async_remote_copy(
+            src_ref=x_ref,
+            dst_ref=own,
+            send_sem=send_sem.at[slot],
+            recv_sem=recv_sem.at[slot],
+            device_id=(peer, adj_index),
+            device_id_type=pl.DeviceIdType.MESH,
+        )
+        for slot, peer in enumerate(peers)
+    ]
+    for copy in copies:
+        copy.start()
+    kept = pltpu.make_async_copy(x_ref, own, local_sem)
+    kept.start()
+    kept.wait()
+    for copy in copies:
+        copy.wait()
+
+
+def gather_dir(value):
+    count = lax.axis_size("dir")
+    rows, columns = value.shape
+    return pl.pallas_call(
+        functools.partial(gather_kernel, count),
+        out_shape=jax.ShapeDtypeStruct((rows * count, columns), value.dtype),
+        in_specs=[pl.BlockSpec(memory_space=pl.ANY)],
+        out_specs=pl.BlockSpec(memory_space=pl.ANY),
+        scratch_shapes=[
+            pltpu.SemaphoreType.DMA(()),
+            pltpu.SemaphoreType.DMA((count - 1,)),
+            pltpu.SemaphoreType.DMA((count - 1,)),
+        ],
+        compiler_params=pltpu.CompilerParams(collective_id=3),
+        name="gather_dir",
+    )(value)
+
+
 def sum_over(value, axis):
     count = lax.axis_size(axis)
     pair = 2 if axis == "adj" else 1
@@ -210,8 +259,9 @@
     share_rows = direct_snapshots.shape[0] // adj_count
     dir_count = lax.axis_size("dir")
     turned = lax.all_to_all(adjoint_snapshots, "dir", split_axis=1, concat_axis=0, tiled=True)
+    turned, direct_later = lax.optimization_barrier((turned, direct_snapshots))
     gathered = lax.all_gather(turned, "adj", axis=1, tiled=True)
-    direct_whole = lax.all_gather(direct_snapshots, "dir", axis=0, tiled=True)
+    direct_whole = gather_dir(direct_later)
     hankel_tile = dot_t(gathered, direct_whole, ((0,), (0,)), None)
     right_raw = start_block(
         start_seeds, adj_index * direct_snapshots.shape[1], direct_snapshots.shape[1]

time: 663 us -> 620 us (0.935)
  waiting for transfers between devices: 236 us -> 152 us
  Pallas kernels: 320 us -> 367 us
    all_gather x1, waiting for transfers between devices: 84.1 us -> 35.2 us  [local(): gathered = lax.all_gather(turned, 'adj', axis=1, tiled=True)]
    pallas_call x0 -> x1, Pallas kernels: none -> 47 us  [gather_dir(): pl.pallas_call(functools.partial(gather_kernel, count), out_shape=jax.Sha...]
    all_gather x1 -> x0, waiting for transfers between devices: 34.2 us -> none  [local(): direct_whole = lax.all_gather(direct_snapshots, 'dir', axis=0, tiled=True)]
  transfers between devices with their start and end apart: 8 -> 7, of which waited for: 6 -> 5; matrix products, arithmetic and copies ran while one was open for 1% -> 1% of each run, Pallas kernels for 32% -> 42%
where the time goes in v4:
time: 620 us; the launch traced here: 612 us
  Pallas kernels  367 us (59%)
  waiting for transfers between devices  152 us (25%)
  matrix products  51.6 us (8%)
  blocking collectives  19.1 us (3%)
  between operations  14.8 us (2%)
    pallas_call x4, Pallas kernels, factor_inverse(): pl.pallas_call(factor_kernel, out_shape=shape, in_specs=[pl.BlockSpec(mem...  212 us
    pallas_call x4, Pallas kernels, sum_over(): pl.pallas_call(functools.partial(sum_kernel, axis, pair, count), out_shap...  109 us
    psum x1, waiting for transfers between devices, local(): left_raw = lax.psum(product(hankel_tile, right_raw), 'adj')  63.3 us
    pallas_call x1, Pallas kernels, gather_dir(): pl.pallas_call(functools.partial(gather_kernel, count), out_shape=jax.Sha...  47 us
    dot_general x14, matrix products, dot_t(): lax.dot_general(a, b, (dims, ((), ())), precision=precision, preferred_el...  46.6 us
    reduce_scatter x1, waiting for transfers between devices, local(): lax.psum_scatter(jnp.dot(direct_snapshots, right_coarse, preferred_elemen...  38.9 us
    all_gather x1, waiting for transfers between devices, local(): gathered = lax.all_gather(turned, 'adj', axis=1, tiled=True)  35.2 us
    all_to_all x1, blocking collectives, local(): lax.all_to_all(adjoint_snapshots, 'dir', split_axis=1, concat_axis=0, til...  19.1 us
  transfers between devices with their start and end apart: 7, of which 5 were waited for; matrix products, arithmetic and copies ran while one was open for 1% of the time, Pallas kernels for 42%

profile of v4, /device:TPU:0, one launch (start us, length us, event | category | flops | bytes accessed | tf_op | source)
XLA Modules:
  0.0 611.8 jit_solution(12536706848112231668)
XLA Ops:
  7.2 1.5 copy.7
  8.7 19.1 %all_to_all.19 = bf16[1024,4,128]{0,2,1:T(8,128)(2,1)S(1)} all-to-all(bf16[1024,4,128]{0,2,1:T(8,128)(2,1)S(1)} %bitcast.40), channel_id=1, replica_groups=mesh['dir'=4,'adj'=8] {'dir'}, dimensions={1} | all-to-all | bytes 2097152 | tf_op jit(solution)/shard_map/all_to_all | solution.py:261
  29.3 47.0 %gather_dir.1 = bf16[4096,512]{1,0:T(8,128)(2,1)} custom-call(bf16[1024,512]{1,0:T(8,128)(2,1)} %x_ref), custom_call_target="tpu_custom_call" | custom-call | tf_op jit(solution)/shard_map/gather_dir/pallas_call | solution.py:211
  76.3 35.2 %all-gather.2.cloned.1.call-done = bf16[4096,1024]{1,0:T(8,128)(2,1)} async-done(((bf16[4096,128]{1,0:T(8,128)(2,1)}), bf16[4096,1024]{1,0:T(8,128)(2,1)}) %all-gather.2.cloned.1.call-update) | async-done | bytes 8388624 | tf_op jit(solution)/shard_map/all_gather | solution.py:263
  111.6 8.2 %fusion.37 = f32[1024,512]{1,0:T(8,128)S(1)} fusion(bf16[4096,1024]{1,0:T(8,128)(2,1)} %all-gather.2.cloned.1.call-done, bf16[4096,512]{1,0:T(8,128)(2,1)} %gather_dir.1), kind=kOutput, calls=%fused_computation.49 | convolution fusion | flops 4294967296 | bytes 14680064 | tf_op jit(solution)/shard_map/dot_general | solution.py:26
  119.8 4.5 fusion.5
  124.3 63.3 %all-reduce.5.cloned.1.call-done = f32[1024,512]{1,0:T(8,128)} async-done(((f32[1024,512]{1,0:T(8,128)}), f32[1024,512]{1,0:T(8,128)}) %all-reduce.5.cloned.1.call-update) | async-done | bytes 2097168 | tf_op jit(solution)/shard_map/psum | solution.py:269
  187.6 5.7 fusion.38.x_ref
  193.3 25.4 %gram_sum_dir.2.gram_ref = f32[512,512]{1,0:T(8,128)S(1)} custom-call(f32[512,512]{1,0:T(8,128)S(1)} %fusion.38.x_ref), custom_call_target="tpu_custom_call" | custom-call | tf_op jit(solution)/shard_map/gram_sum_dir/pallas_call | solution.py:232
  218.7 2.8 fusion.39
  221.9 52.8 %cholesky_inverse.4 = f32[512,512]{1,0:T(8,128)S(1)} custom-call(f32[512,512]{1,0:T(8,128)S(1)} %gram_sum_dir.2.gram_ref), custom_call_target="tpu_custom_call" | custom-call | tf_op jit(solution)/shard_map/cholesky_inverse/pallas_call | solution.py:90
  274.9 2.4 fusion.40
  277.3 3.2 fusion.42
  280.5 1.9 fusion.41.x_ref
  282.4 29.1 %gram_sum_adj.2.gram_ref = f32[512,512]{1,0:T(8,128)S(1)} custom-call(f32[512,512]{1,0:T(8,128)S(1)} %fusion.41.x_ref), custom_call_target="tpu_custom_call" | custom-call | tf_op jit(solution)/shard_map/gram_sum_adj/pallas_call | solution.py:232
  312.0 52.9 %cholesky_inverse.5 = f32[512,512]{1,0:T(8,128)S(1)} custom-call(f32[512,512]{1,0:T(8,128)S(1)} %gram_sum_adj.2.gram_ref), custom_call_target="tpu_custom_call" | custom-call | tf_op jit(solution)/shard_map/cholesky_inverse/pallas_call | solution.py:90
  365.0 13.8 %all-reduce.9.cloned.1.call-done = f32[1024,512]{1,0:T(8,128)} async-done(((f32[1024,512]{1,0:T(8,128)}), f32[1024,512]{1,0:T(8,128)}) %all-reduce.9.cloned.1.call-update) | async-done | bytes 2097168 | tf_op jit(solution)/shard_map/psum | solution.py:253
  378.8 3.6 fusion.43
  382.4 2.9 fusion.45
  385.3 3.5 fusion.44.x_ref
  388.9 26.0 %gram_sum_dir.3.gram_ref = f32[512,512]{1,0:T(8,128)S(1)} custom-call(f32[512,512]{1,0:T(8,128)S(1)} %fusion.44.x_ref), custom_call_target="tpu_custom_call" | custom-call | tf_op jit(solution)/shard_map/gram_sum_dir/pallas_call | solution.py:232
  414.9 1.5 constant_dynamic-slice_fusion
  416.4 53.0 %cholesky_inverse.6 = f32[512,512]{1,0:T(8,128)S(1)} custom-call(f32[512,512]{1,0:T(8,128)S(1)} %gram_sum_dir.3.gram_ref), custom_call_target="tpu_custom_call" | custom-call | tf_op jit(solution)/shard_map/cholesky_inverse/pallas_call | solution.py:90
  469.4 2.8 convolution_convert_fusion
  472.2 2.3 fusion.46
  474.5 1.9 fusion.47.x_ref
  476.3 28.3 %gram_sum_adj.3.gram_ref = f32[512,512]{1,0:T(8,128)S(1)} custom-call(f32[512,512]{1,0:T(8,128)S(1)} %fusion.47.x_ref), custom_call_target="tpu_custom_call" | custom-call | tf_op jit(solution)/shard_map/gram_sum_adj/pallas_call | solution.py:232
  504.6 1.7 fusion.48
  506.4 53.0 %cholesky_inverse.7 = f32[512,512]{1,0:T(8,128)S(1)} custom-call(f32[512,512]{1,0:T(8,128)S(1)} %gram_sum_adj.3.gram_ref), custom_call_target="tpu_custom_call" | custom-call | tf_op jit(solution)/shard_map/cholesky_inverse/pallas_call | solution.py:90
  560.5 3.3 convolution_bitcast_fusion
  563.8 38.9 %reduce-scatter.5.cloned.1.call-done = f32[128,512]{0,1:T(8,128)} async-done(((f32[1024,512]{0,1:T(8,128)}), f32[128,512]{0,1:T(8,128)}) %reduce-scatter.5.cloned.1.call-update) | async-done | bytes 262160 | tf_op jit(solution)/shard_map/reduce_scatter | solution.py:299
  602.7 1.8 copy.9
  (38 shorter events, 4.0 us)
Async XLA Ops:
  7.2 104.4 %all-gather.2.cloned.1.call-start = ((), (), s32[]{:S(2)}) async-start(), calls=%async_computation.3 | async-start | bytes 9437184 | tf_op jit(solution)/shard_map/all_gather | solution.py:263
  27.8 1.5 copy-start.7
  29.2 158.4 %all-reduce.5.cloned.1.call-start = ((), (), s32[]{:S(2)}) async-start(), calls=%async_computation.4 | async-start | bytes 4194304 | tf_op jit(solution)/shard_map/psum | solution.py:269
  119.8 98.9 %copy-start.3 = (f32[1024,512]{1,0:T(8,128)}, f32[1024,512]{1,0:T(8,128)S(1)}, u32[]{:S(2)}) copy-start(f32[1024,512]{1,0:T(8,128)S(1)} %fusion.37) | copy-start | bytes 6291460
  124.2 150.7 %all-reduce.7.cloned.1.call-start = ((), (), s32[]{:S(2)}) async-start(), calls=%async_computation.5 | async-start | bytes 2097152 | tf_op jit(solution)/shard_map/psum | solution.py:253
  193.3 25.4 %copy-start.2 = (f32[1024,512]{1,0:T(8,128)S(1)}, f32[1024,512]{1,0:T(8,128)}, u32[]{:S(2)}) copy-start(f32[1024,512]{1,0:T(8,128)} %all-reduce.5.cloned.1.call-done) | copy-start | bytes 6291460
  221.6 157.2 %all-reduce.9.cloned.1.call-start = ((), (), s32[]{:S(2)}) async-start(), calls=%async_computation.6 | async-start | bytes 4194304 | tf_op jit(solution)/shard_map/psum | solution.py:253
  274.9 2.4 copy-start.4
  311.5 160.7 %all-reduce.11.cloned.1.call-start = ((), (), s32[]{:S(2)}) async-start(), calls=%async_computation.7 | async-start | bytes 2097152 | tf_op jit(solution)/shard_map/psum | solution.py:253
  378.8 3.6 copy-start.5
  382.4 3.0 copy-start
  414.9 144.5 %reduce-scatter.3.cloned.1.call-start = ((), (), s32[]{:S(2)}) async-start(), calls=%async_computation.8 | async-start | bytes 1310720 | tf_op jit(solution)/shard_map/reduce_scatter | solution.py:287
  414.9 54.4 %copy-start.1 = (f32[1024,512]{1,0:T(8,128)S(1)}, f32[1024,512]{1,0:T(8,128)}, u32[]{:S(2)}) copy-start(f32[1024,512]{1,0:T(8,128)} %copy-done) | copy-start | bytes 6291460
  474.5 30.2 %copy-start.6 = (bf16[1024,512]{1,0:T(8,128)(2,1)S(1)}, bf16[1024,512]{1,0:T(8,128)(2,1)}, u32[]{:S(2)}) copy-start(bf16[1024,512]{1,0:T(8,128)(2,1)} %convolution_convert_fusion) | copy-start | bytes 3145732
  506.3 96.4 %reduce-scatter.5.cloned.1.call-start = ((), (), s32[]{:S(2)}) async-start(), calls=%async_computation.9 | async-start | bytes 2359296 | tf_op jit(solution)/shard_map/reduce_scatter | solution.py:299
Sparse Core Ops, SparseCore 0:
  29.3 82.2 all-gather.1
  124.4 63.1 all-reduce.4
  221.7 53.1 all-reduce.6
  311.6 67.1 all-reduce.8
  415.0 53.0 all-reduce.10
  506.5 30.8 reduce-scatter.2
  563.9 38.7 reduce-scatter.4
